TPU v7x, 32 devices: a whole 2x2x4 slice. The times are simulated.
32 devices in a mesh: dp: 16 (over z, y, x), head: 2 (over core).
Axes of the slice: x: 2, y: 2, z: 4, core: 2. Of those that a mesh axis runs over, the one named last changes fastest.
Arguments:
- tokens: bfloat16 [8192, 768], P('dp'), may hold values from -6 to 6
- memory: bfloat16 [32768, 768], P(('dp', 'head')), may hold values from -12 to 12
- cotangent: bfloat16 [8192, 768], P('dp'), may hold values from -12 to 12
- patch_item: int32 [32768], P('dp'), may hold values from 0 to 3, as said below
- patch_mask: int32 [32768], P('dp'), may hold values from 0 to 1, as said below
- text_item: int32 [32], P('dp'), may hold values from 0 to 3, as said below
- text_len: int32 [32], P('dp'), may hold values from 1 to 256
- norm_gains: float32 [3, 768], P(None, 'dp'), may hold values from 0.3 to 2.3
- gains_mean: float32 [3, 768], P(None, 'dp'), may hold values from -0.001953125 to 0.001953125
- gains_square: float32 [3, 768], P(None, 'dp'), may hold values from 4.4493937e-08 to 3.6018903e-07
- self_proj: float32 [3, 768, 768], P(None, 'dp', 'head'), may hold values from -0.21875 to 0.21875
- self_proj_mean: float32 [3, 768, 768], P(None, 'dp', 'head'), may hold values from -0.00048828125 to 0.00048828125
- self_proj_square: float32 [3, 768, 768], P(None, 'dp', 'head'), may hold values from 2.7543867e-09 to 2.2246969e-08
- query_cross: float32 [768, 768], P('dp', 'head'), may hold values from -0.21875 to 0.21875
- query_cross_mean: float32 [768, 768], P('dp', 'head'), may hold values from -0.00048828125 to 0.00048828125
- query_cross_square: float32 [768, 768], P('dp', 'head'), may hold values from 2.7543867e-09 to 2.2246969e-08
- keyval_cross: float32 [2, 768, 768], P(None, ('dp', 'head')), may hold values from -0.21875 to 0.21875
- keyval_cross_mean: float32 [2, 768, 768], P(None, ('dp', 'head')), may hold values from -0.00048828125 to 0.00048828125
- keyval_cross_square: float32 [2, 768, 768], P(None, ('dp', 'head')), may hold values from 2.7543867e-09 to 2.2246969e-08
- out_proj: float32 [2, 768, 768], P(None, 'head', 'dp'), may hold values from -0.875 to 0.875
- out_proj_mean: float32 [2, 768, 768], P(None, 'head', 'dp'), may hold values from -0.00048828125 to 0.00048828125
- out_proj_square: float32 [2, 768, 768], P(None, 'head', 'dp'), may hold values from 2.7543867e-09 to 2.2246969e-08
- mlp_input: float32 [2, 768, 2048], P(None, 'dp', 'head'), may hold values from -0.21875 to 0.21875
- mlp_input_mean: float32 [2, 768, 2048], P(None, 'dp', 'head'), may hold values from -0.00048828125 to 0.00048828125
- mlp_input_square: float32 [2, 768, 2048], P(None, 'dp', 'head'), may hold values from 2.7543867e-09 to 2.2246969e-08
- mlp_output: float32 [2048, 768], P('head', 'dp'), may hold values from -0.125 to 0.125
- mlp_output_mean: float32 [2048, 768], P('head', 'dp'), may hold values from -0.00048828125 to 0.00048828125
- mlp_output_square: float32 [2048, 768], P('head', 'dp'), may hold values from 2.7543867e-09 to 2.2246969e-08
Outputs:
- output: bfloat16 [8192, 768], P('dp')
- tokens_grad: float32 [8192, 768], P('dp')
- memory_grad: float32 [32768, 768], P(('dp', 'head'))
- grad_norm: float32 [], replicated
- new_gains: float32 [3, 768], P(None, 'dp')
- new_gains_mean: float32 [3, 768], P(None, 'dp')
- new_gains_square: float32 [3, 768], P(None, 'dp')
- new_self_proj: float32 [3, 768, 768], P(None, 'dp', 'head')
- new_self_proj_mean: float32 [3, 768, 768], P(None, 'dp', 'head')
- new_self_proj_square: float32 [3, 768, 768], P(None, 'dp', 'head')
- new_query_cross: float32 [768, 768], P('dp', 'head')
- new_query_cross_mean: float32 [768, 768], P('dp', 'head')
- new_query_cross_square: float32 [768, 768], P('dp', 'head')
- new_keyval_cross: float32 [2, 768, 768], P(None, ('dp', 'head'))
- new_keyval_cross_mean: float32 [2, 768, 768], P(None, ('dp', 'head'))
- new_keyval_cross_square: float32 [2, 768, 768], P(None, ('dp', 'head'))
- new_out_proj: float32 [2, 768, 768], P(None, 'head', 'dp')
- new_out_proj_mean: float32 [2, 768, 768], P(None, 'head', 'dp')
- new_out_proj_square: float32 [2, 768, 768], P(None, 'head', 'dp')
- new_mlp_input: float32 [2, 768, 2048], P(None, 'dp', 'head')
- new_mlp_input_mean: float32 [2, 768, 2048], P(None, 'dp', 'head')
- new_mlp_input_square: float32 [2, 768, 2048], P(None, 'dp', 'head')
- new_mlp_output: float32 [2048, 768], P('head', 'dp')
- new_mlp_output_mean: float32 [2048, 768], P('head', 'dp')
- new_mlp_output_square: float32 [2048, 768], P('head', 'dp')
Inputs may be any that keep to these rules, and one draw needn't show every extreme that they name: `patch_item`: each group of 2048 patches consists of units of 512 patches; its items take 1, 2 or 4 units, are aligned to their size and never cross a boundary of 4 units; every patch holds the first unit of its item, counted from 0 within the group. `patch_mask`: the first patch of every unit is 1. `text_item`: text s holds the first unit of one of the items of group s // 2.
All inputs are finite; a program needn't handle non-finite values.
Results may differ from a plain program's by a relative error of at most 0.03.
Values may be sent and summed in bfloat16 or wider, within the bound.
A program may use at most 128 MiB of HBM per device.

v0:
```python
import jax
import jax.numpy as jnp
from jax import lax
from jax.sharding import PartitionSpec as P

D = 768
HD = 64
FF = 2048
TXT = 256
STEP = 10


BETA1 = 0.9
BETA2 = 0.95
ADAM_EPS = 1e-08
DECAY = 0.1
CLIP = 1.0
NORM_EPS = 1e-06
MASKED = -1e30


def rms_gain(values, gain):
    inverse = lax.rsqrt(jnp.mean(values * values, axis=-1, keepdims=True) + NORM_EPS)
    return values * inverse * gain


def gated(gate, up_part):
    return jax.nn.gelu(gate, approximate=True) * up_part


def head_total(partial_value):
    return lax.psum(partial_value.astype(jnp.bfloat16), "head").astype(jnp.float32)


def text_masks(text_len):
    place = jnp.arange(TXT, dtype=jnp.int32)
    causal = place[None, :] <= place[:, None]
    return causal[None, :, :] & (place[None, None, :] < text_len[:, None, None])


def cross_masks(text_item, patch_item, patch_mask, count_rows):
    positions = jnp.arange(count_rows, dtype=jnp.int32)
    sequence = positions // TXT
    slots = jnp.arange(text_item.shape[0], dtype=jnp.int32)
    member = sequence[:, None] == slots[None, :]
    own_item = jnp.sum(jnp.where(member, text_item[None, :], 0), axis=1)
    return (own_item[:, None] == patch_item[None, :]) & (patch_mask[None, :] == 1)


def masked_scores(query, keys, allowed, start):
    query_head = lax.dynamic_slice_in_dim(query, start, HD, 1)
    key_head = lax.dynamic_slice_in_dim(keys, start, HD, 1)
    scores = jnp.einsum(
        "qd,kd->qk", query_head, key_head, preferred_element_type=jnp.float32
    ) * HD ** (-0.5)
    return (jnp.where(allowed, scores, MASKED), query_head, key_head)


def attention_forward(query, keys, values, allowed):
    width = query.shape[1]
    heads = width // HD

    def one_head(index, carry):
        outputs, logsum = carry
        start = index * HD
        scores, query_head, key_head = masked_scores(query, keys, allowed, start)
        value_head = lax.dynamic_slice_in_dim(values, start, HD, 1)
        highest = jnp.max(scores, axis=1, keepdims=True)
        expo = jnp.exp(scores - highest)
        total = jnp.sum(expo, axis=1, keepdims=True)
        probs = (expo / total).astype(jnp.bfloat16)
        result = jnp.dot(probs, value_head, preferred_element_type=jnp.float32)
        outputs = lax.dynamic_update_slice_in_dim(outputs, result, start, 1)
        logsum = lax.dynamic_update_slice_in_dim(logsum, highest + jnp.log(total), index, 1)
        return (outputs, logsum)

    start_state = (
        jnp.zeros((query.shape[0], width), jnp.float32),
        jnp.zeros((query.shape[0], heads), jnp.float32),
    )
    return lax.fori_loop(0, heads, one_head, start_state)


def attention_backward(query, keys, values, allowed, logsum, grad_mixed):
    width = query.shape[1]
    heads = width // HD
    scale = HD ** (-0.5)

    def one_head(index, carry):
        grad_query, grad_keys, grad_values = carry
        start = index * HD
        scores, query_head, key_head = masked_scores(query, keys, allowed, start)
        value_head = lax.dynamic_slice_in_dim(values, start, HD, 1)
        grad_head = lax.dynamic_slice_in_dim(grad_mixed, start, HD, 1)
        probs = jnp.exp(scores - lax.dynamic_slice_in_dim(logsum, index, 1, 1))
        grad_value = jnp.einsum(
            "qk,qd->kd", probs.astype(jnp.bfloat16), grad_head, preferred_element_type=jnp.float32
        )
        grad_probs = jnp.einsum(
            "qd,kd->qk", grad_head, value_head, preferred_element_type=jnp.float32
        )
        inner = jnp.sum(grad_probs * probs, axis=1, keepdims=True)
        grad_scores = (probs * (grad_probs - inner)).astype(jnp.bfloat16)
        grad_q = jnp.dot(grad_scores, key_head, preferred_element_type=jnp.float32) * scale
        grad_k = (
            jnp.einsum("qk,qd->kd", grad_scores, query_head, preferred_element_type=jnp.float32)
            * scale
        )
        grad_query = lax.dynamic_update_slice_in_dim(grad_query, grad_q, start, 1)
        grad_keys = lax.dynamic_update_slice_in_dim(grad_keys, grad_k, start, 1)
        grad_values = lax.dynamic_update_slice_in_dim(grad_values, grad_value, start, 1)
        return (grad_query, grad_keys, grad_values)

    start_state = (
        jnp.zeros(query.shape, jnp.float32),
        jnp.zeros(keys.shape, jnp.float32),
        jnp.zeros(values.shape, jnp.float32),
    )
    return lax.fori_loop(0, heads, one_head, start_state)


def by_text(array):
    return array.reshape(array.shape[0] // TXT, TXT, array.shape[1])


def by_rows(array):
    return array.reshape(array.shape[0] * array.shape[1], array.shape[2])


def project_memory(memory, keyval):
    local = jnp.einsum("pd,jde->pje", memory, keyval, preferred_element_type=jnp.float32).astype(
        jnp.bfloat16
    )
    groups = lax.axis_size("head")
    return local.reshape(local.shape[0], 2, groups, local.shape[2] // groups)


def split_heads(stacked):
    return (stacked[:, 0, 0, :], stacked[:, 1, 0, :])


def adam_step(weight, first, second, grad, rate, decay):
    first_new = BETA1 * first + (1.0 - BETA1) * grad
    second_new = BETA2 * second + (1.0 - BETA2) * grad * grad
    mean_hat = first_new / (1.0 - BETA1**STEP)
    square_hat = second_new / (1.0 - BETA2**STEP)
    weight_new = weight - rate * (mean_hat / (jnp.sqrt(square_hat) + ADAM_EPS) + decay * weight)
    return (weight_new, first_new, second_new)


def per_device(
    tokens,
    memory,
    cotangent,
    patch_item,
    patch_mask,
    text_item,
    text_len,
    norm_gains,
    gains_mean,
    gains_square,
    self_proj,
    self_proj_mean,
    self_proj_square,
    query_cross,
    query_cross_mean,
    query_cross_square,
    keyval_cross,
    keyval_cross_mean,
    keyval_cross_square,
    out_proj,
    out_proj_mean,
    out_proj_square,
    mlp_input,
    mlp_input_mean,
    mlp_input_square,
    mlp_output,
    mlp_output_mean,
    mlp_output_square,
):
    gathered = (
        lax.all_gather(norm_gains.astype(jnp.bfloat16), "dp", axis=1, tiled=True),
        lax.all_gather(self_proj.astype(jnp.bfloat16), "dp", axis=1, tiled=True),
        lax.all_gather(query_cross.astype(jnp.bfloat16), "dp", axis=0, tiled=True),
        lax.all_gather(out_proj.astype(jnp.bfloat16), "dp", axis=2, tiled=True),
        lax.all_gather(mlp_input.astype(jnp.bfloat16), "dp", axis=1, tiled=True),
        lax.all_gather(mlp_output.astype(jnp.bfloat16), "dp", axis=1, tiled=True),
    )
    gain_full, self_full, query_full, out_full, input_full, output_full = gathered
    keyval_full = lax.all_gather(
        keyval_cross.astype(jnp.bfloat16), ("dp", "head"), axis=1, tiled=True
    )
    gain_values = gain_full.astype(jnp.float32)
    self_allowed = text_masks(text_len)
    cross_allowed = cross_masks(text_item, patch_item, patch_mask, tokens.shape[0])
    residual_in = tokens.astype(jnp.float32)
    normed_one = rms_gain(residual_in, gain_values[0]).astype(jnp.bfloat16)
    projected = jnp.einsum(
        "td,jdh->jth", normed_one, self_full, preferred_element_type=jnp.float32
    ).astype(jnp.bfloat16)
    query, keys, values = (projected[0], projected[1], projected[2])
    attended, self_logsum = jax.vmap(attention_forward)(
        by_text(query), by_text(keys), by_text(values), self_allowed
    )
    attended = by_rows(attended).astype(jnp.bfloat16)
    first = residual_in + head_total(
        jnp.dot(attended, out_full[0], preferred_element_type=jnp.float32)
    )
    normed_two = rms_gain(first, gain_values[1]).astype(jnp.bfloat16)
    cross_query = jnp.dot(normed_two, query_full, preferred_element_type=jnp.float32).astype(
        jnp.bfloat16
    )
    arrived = lax.all_to_all(
        project_memory(memory, keyval_full), "head", split_axis=2, concat_axis=0, tiled=True
    )
    memory_keys, memory_values = split_heads(arrived)
    mixed, cross_logsum = attention_forward(cross_query, memory_keys, memory_values, cross_allowed)
    mixed = mixed.astype(jnp.bfloat16)
    second = first + head_total(jnp.dot(mixed, out_full[1], preferred_element_type=jnp.float32))
    normed_three = rms_gain(second, gain_values[2]).astype(jnp.bfloat16)
    gate = jnp.dot(normed_three, input_full[0], preferred_element_type=jnp.float32)
    up_part = jnp.dot(normed_three, input_full[1], preferred_element_type=jnp.float32)
    hidden = gated(gate, up_part).astype(jnp.bfloat16)
    output = second + head_total(jnp.dot(hidden, output_full, preferred_element_type=jnp.float32))
    grad_hidden = jnp.einsum(
        "td,fd->tf", cotangent, output_full, preferred_element_type=jnp.float32
    )
    grad_mlp_output = jnp.einsum("tf,td->fd", hidden, cotangent, preferred_element_type=jnp.float32)
    gated_value, gated_pull = jax.vjp(gated, gate, up_part)
    grad_gate, grad_up = gated_pull(grad_hidden)
    grad_gate = grad_gate.astype(jnp.bfloat16)
    grad_up = grad_up.astype(jnp.bfloat16)
    grad_mlp_input = jnp.stack(
        [
            jnp.einsum("td,tf->df", normed_three, grad_gate, preferred_element_type=jnp.float32),
            jnp.einsum("td,tf->df", normed_three, grad_up, preferred_element_type=jnp.float32),
        ]
    )
    grad_normed_three = head_total(
        jnp.einsum("tf,df->td", grad_gate, input_full[0], preferred_element_type=jnp.float32)
        + jnp.einsum("tf,df->td", grad_up, input_full[1], preferred_element_type=jnp.float32)
    )
    norm_value, norm_pull = jax.vjp(rms_gain, second, gain_values[2])
    grad_second_norm, grad_gain_three = norm_pull(grad_normed_three)
    grad_second = cotangent.astype(jnp.float32) + grad_second_norm
    grad_cross_branch = grad_second.astype(jnp.bfloat16)
    grad_mixed = jnp.einsum(
        "td,hd->th", grad_cross_branch, out_full[1], preferred_element_type=jnp.float32
    ).astype(jnp.bfloat16)
    grad_out_cross = jnp.einsum(
        "th,td->hd", mixed, grad_cross_branch, preferred_element_type=jnp.float32
    )
    again = lax.all_to_all(
        project_memory(memory, keyval_full), "head", split_axis=2, concat_axis=0, tiled=True
    )
    back_keys, back_values = split_heads(again)
    grad_cross_query, grad_memory_keys, grad_memory_values = attention_backward(
        cross_query, back_keys, back_values, cross_allowed, cross_logsum, grad_mixed
    )
    grad_cross_query = grad_cross_query.astype(jnp.bfloat16)
    grad_query_cross = jnp.einsum(
        "td,th->dh", normed_two, grad_cross_query, preferred_element_type=jnp.float32
    )
    sent_back = jnp.stack([grad_memory_keys, grad_memory_values], axis=1).astype(jnp.bfloat16)[
        :, :, None, :
    ]
    returned = lax.all_to_all(sent_back, "head", split_axis=0, concat_axis=2, tiled=True)
    returned = returned.reshape(returned.shape[0], 2, returned.shape[2] * returned.shape[3])
    memory_grad = jnp.einsum(
        "pje,jde->pd", returned, keyval_full, preferred_element_type=jnp.float32
    )
    grad_keyval = jnp.einsum("pd,pje->jde", memory, returned, preferred_element_type=jnp.float32)
    keyval_reduced = lax.psum_scatter(grad_keyval, ("dp", "head"), scatter_dimension=1, tiled=True)
    grad_normed_two = head_total(
        jnp.einsum("th,dh->td", grad_cross_query, query_full, preferred_element_type=jnp.float32)
    )
    norm_value, norm_pull = jax.vjp(rms_gain, first, gain_values[1])
    grad_first_norm, grad_gain_two = norm_pull(grad_normed_two)
    grad_first = grad_second + grad_first_norm
    grad_self_branch = grad_first.astype(jnp.bfloat16)
    grad_attended = jnp.einsum(
        "td,hd->th", grad_self_branch, out_full[0], preferred_element_type=jnp.float32
    ).astype(jnp.bfloat16)
    grad_out_self = jnp.einsum(
        "th,td->hd", attended, grad_self_branch, preferred_element_type=jnp.float32
    )
    grad_query, grad_keys, grad_values = jax.vmap(attention_backward)(
        by_text(query),
        by_text(keys),
        by_text(values),
        self_allowed,
        self_logsum,
        by_text(grad_attended),
    )
    grad_projected = jnp.stack(
        [by_rows(grad_query), by_rows(grad_keys), by_rows(grad_values)]
    ).astype(jnp.bfloat16)
    grad_self_proj = jnp.einsum(
        "td,jth->jdh", normed_one, grad_projected, preferred_element_type=jnp.float32
    )
    grad_normed_one = head_total(
        jnp.einsum("jth,jdh->td", grad_projected, self_full, preferred_element_type=jnp.float32)
    )
    norm_value, norm_pull = jax.vjp(rms_gain, residual_in, gain_values[0])
    grad_input_norm, grad_gain_one = norm_pull(grad_normed_one)
    tokens_grad = grad_first + grad_input_norm
    grad_gains = jnp.stack([grad_gain_one, grad_gain_two, grad_gain_three])
    grad_out_proj = jnp.stack([grad_out_self, grad_out_cross])
    reduced = (
        lax.psum_scatter(grad_gains, "dp", scatter_dimension=1, tiled=True),
        lax.psum_scatter(grad_self_proj, "dp", scatter_dimension=1, tiled=True),
        lax.psum_scatter(grad_query_cross, "dp", scatter_dimension=0, tiled=True),
        lax.psum_scatter(grad_out_proj, "dp", scatter_dimension=2, tiled=True),
        lax.psum_scatter(grad_mlp_input, "dp", scatter_dimension=1, tiled=True),
        lax.psum_scatter(grad_mlp_output, "dp", scatter_dimension=1, tiled=True),
    )
    gain_reduced, self_reduced, query_reduced, out_reduced, input_reduced, output_reduced = reduced
    squares = (
        jnp.sum(self_reduced * self_reduced)
        + jnp.sum(query_reduced * query_reduced)
        + jnp.sum(out_reduced * out_reduced)
    )
    squares = (
        squares
        + jnp.sum(input_reduced * input_reduced)
        + jnp.sum(output_reduced * output_reduced)
        + jnp.sum(keyval_reduced * keyval_reduced)
    )
    squares = squares + jnp.where(
        lax.axis_index("head") == 0, jnp.sum(gain_reduced * gain_reduced), 0.0
    )
    total = lax.psum(squares, ("dp", "head"))
    grad_norm = jnp.sqrt(total)
    factor = jnp.minimum(1.0, CLIP / (grad_norm + NORM_EPS))
    wide_rate = 2.0 * D ** (-0.5)
    new_gains = adam_step(norm_gains, gains_mean, gains_square, gain_reduced * factor, 0.5, 0.0)
    new_self = adam_step(
        self_proj, self_proj_mean, self_proj_square, self_reduced * factor, wide_rate, DECAY
    )
    new_query = adam_step(
        query_cross, query_cross_mean, query_cross_square, query_reduced * factor, wide_rate, DECAY
    )
    new_keyval = adam_step(
        keyval_cross,
        keyval_cross_mean,
        keyval_cross_square,
        keyval_reduced * factor,
        wide_rate,
        DECAY,
    )
    new_out = adam_step(
        out_proj,
        out_proj_mean,
        out_proj_square,
        out_reduced * factor,
        2.0 * (D // 16) ** (-0.5),
        DECAY,
    )
    new_input = adam_step(
        mlp_input, mlp_input_mean, mlp_input_square, input_reduced * factor, wide_rate, DECAY
    )
    new_output = adam_step(
        mlp_output,
        mlp_output_mean,
        mlp_output_square,
        output_reduced * factor,
        2.0 * FF ** (-0.5),
        DECAY,
    )
    return (
        output.astype(jnp.bfloat16),
        tokens_grad,
        memory_grad,
        grad_norm,
        new_gains[0],
        new_gains[1],
        new_gains[2],
        new_self[0],
        new_self[1],
        new_self[2],
        new_query[0],
        new_query[1],
        new_query[2],
        new_keyval[0],
        new_keyval[1],
        new_keyval[2],
        new_out[0],
        new_out[1],
        new_out[2],
        new_input[0],
        new_input[1],
        new_input[2],
        new_output[0],
        new_output[1],
        new_output[2],
    )


def solution(mesh):
    in_specs = (
        P("dp", None),
        P(("dp", "head"), None),
        P("dp", None),
        P("dp"),
        P("dp"),
        P("dp"),
        P("dp"),
        P(None, "dp"),
        P(None, "dp"),
        P(None, "dp"),
        P(None, "dp", "head"),
        P(None, "dp", "head"),
        P(None, "dp", "head"),
        P("dp", "head"),
        P("dp", "head"),
        P("dp", "head"),
        P(None, ("dp", "head"), None),
        P(None, ("dp", "head"), None),
        P(None, ("dp", "head"), None),
        P(None, "head", "dp"),
        P(None, "head", "dp"),
        P(None, "head", "dp"),
        P(None, "dp", "head"),
        P(None, "dp", "head"),
        P(None, "dp", "head"),
        P("head", "dp"),
        P("head", "dp"),
        P("head", "dp"),
    )
    out_specs = (
        P("dp", None),
        P("dp", None),
        P(("dp", "head"), None),
        P(),
        P(None, "dp"),
        P(None, "dp"),
        P(None, "dp"),
        P(None, "dp", "head"),
        P(None, "dp", "head"),
        P(None, "dp", "head"),
        P("dp", "head"),
        P("dp", "head"),
        P("dp", "head"),
        P(None, ("dp", "head"), None),
        P(None, ("dp", "head"), None),
        P(None, ("dp", "head"), None),
        P(None, "head", "dp"),
        P(None, "head", "dp"),
        P(None, "head", "dp"),
        P(None, "dp", "head"),
        P(None, "dp", "head"),
        P(None, "dp", "head"),
        P("head", "dp"),
        P("head", "dp"),
        P("head", "dp"),
    )
    return jax.shard_map(
        per_device, mesh=mesh, in_specs=in_specs, out_specs=out_specs, check_vma=False
    )
```

profile of v0, /device:TPU:0, one launch (start us, length us, event | category | flops | bytes accessed | tf_op | source)
XLA Modules:
  0.0 1734.0 jit_solution(9564973761700429744)
XLA Ops:
  12.9 42.4 %all-gather = bf16[16,48,3]{1,2,0:T(4,128)(2,1)S(1)} all-gather(bf16[1,48,3]{1,2,0:T(4,128)(2,1)S(1)} %convert_bitcast_fusion.2), channel_id=1, replica_groups=mesh['dp'=16,'head'=2] {'dp'}, dimensions={0}, use_global_device_ids=true | all-gather | bytes 4896 | tf_op jit(solution)/shard_map/all_gather | solution.py:182
  58.1 15.9 all-gather.7.cloned.1.call-done
  79.7 60.5 %while.81 = (s32[]{:T(128)}, bf16[2,256,384]{1,2,0:T(8,128)(2,1)S(1)}, f32[2,256,6]{1,0,2:T(2,128)S(1)}, bf16[2,256,384]{1,2,0:T(8,128)(2,1)}, bf16[2,256,384]{1...) while((s32[]{:T(128)}, ...), condition=%wide.region_6.7_spmd.clone, body=%wide.region_1.6_spmd.clone.sunk | while | flops 34766896 | bytes 2119482 | solution.py:81
  145.9 44.9 %all_gather.24 = bf16[768,384]{1,0:T(8,128)(2,1)} all-gather(bf16[48,384]{1,0:T(8,128)(2,1)S(1)} %convert_element_type.189), channel_id=1, replica_groups=mesh['dp'=16,'head'=2] {'dp'}, dimensions={0}, use_global_device_ids=true | all-gather | bytes 626688 | tf_op jit(solution)/shard_map/all_gather | solution.py:184
  193.8 11.4 all-gather.11.cloned.1.call-done
  205.2 4.6 convolution_convert_fusion
  210.1 7.3 all_to_all.38
  217.4 4.6 copy.336
  222.0 3.9 slice_bitcast_fusion.2
  225.9 54.8 %while.82 = (s32[]{:T(128)}, bf16[512,384]{0,1:T(8,128)(2,1)S(1)}, f32[512,6]{0,1:T(8,128)}, bf16[512,384]{1,0:T(8,128)(2,1)}, bf16[2048,384]{1,0:T(8,128)(2,1)}...) while((s32[]{:T(128)}, bf16[512,384]{0,1:T(8,128)(2,1)S(1)}, ...), condition=%wide.region_13.14_spmd.clone, body=%wide.region_10.13_spmd.clone.sunk | while | flops 278920704 | bytes 30705868 | solution.py:81
  231.7 3.4 fusion.205
  240.8 3.4 fusion.205
  249.9 3.4 fusion.205
  259.1 3.4 fusion.205
  268.2 3.4 fusion.205
  277.3 3.4 fusion.205
  287.4 14.3 all-reduce.15.cloned.1.call-done
  305.5 68.7 %all-gather.13.cloned.1.call-done = bf16[2,768,1024]{2,1,0:T(8,128)(2,1)} async-done(((bf16[2,48,1024]{2,1,0:T(8,128)(2,1)}), bf16[2,768,1024]{2,1,0:T(8,128)(2,1)}) %all-gather.13.cloned.1.call-update) | async-done | bytes 3145744 | tf_op jit(solution)/shard_map/all_gather | solution.py:186
  374.2 4.1 fusion.91
  380.6 53.2 %all-gather.15.cloned.1.call-done = bf16[1024,768]{0,1:T(8,128)(2,1)} async-done(((bf16[1024,48]{0,1:T(8,128)(2,1)}), bf16[1024,768]{0,1:T(8,128)(2,1)}) %all-gather.15.cloned.1.call-update) | async-done | bytes 1572880 | tf_op jit(solution)/shard_map/all_gather | solution.py:187
  433.8 6.4 multiply_convert_fusion.2
  443.5 18.1 %all-reduce.17.cloned.1.call-done = bf16[512,768]{1,0:T(8,128)(2,1)} async-done(((bf16[512,768]{1,0:T(8,128)(2,1)}), bf16[512,768]{1,0:T(8,128)(2,1)}) %all-reduce.17.cloned.1.call-update) | async-done | bytes 786448 | tf_op jit(solution)/shard_map/psum | solution.py:32
  469.8 71.0 %while.83 = (s32[]{:T(128)}, bf16[512,384]{0,1:T(8,128)(2,1)}, bf16[2048,384]{0,1:T(8,128)(2,1)}, bf16[2048,384]{0,1:T(8,128)(2,1)}, bf16[512,384]{1,0:T(8,128)(...) while((s32[]{:T(128)}, bf16[512,384]{0,1:T(8,128)(2,1)}, ...), condition=%wide.region_21.22_spmd.clone, body=%wide.region_19.21_spmd.clone.sunk | while | flops 682786304 | bytes 34761928 | solution.py:119
  543.7 3.6 convolution_convert_fusion.2
  547.4 16.7 all-reduce.19.cloned.1.call-done
  571.8 142.0 %while.84 = (s32[]{:T(128)}, bf16[2,256,384]{1,2,0:T(8,128)(2,1)}, bf16[2,256,384]{1,2,0:T(8,128)(2,1)}, bf16[2,256,384]{1,2,0:T(8,128)(2,1)}, bf16[2,256,384]{1...) while((s32[]{:T(128)}, bf16[2,256,384]{1,2,0:T(8,128)(2,1)}, ...), condition=%wide.region_27.28_spmd.clone, body=%wide.region_24.27_spmd.clone.sunk | while | flops 85360160 | bytes 5260600 | solution.py:119
  627.1 3.1 fusion.227
  637.7 3.1 convolution_select_fusion.5
  685.2 3.1 convolution_select_fusion.5
  717.4 3.8 bitcast_convert_fusion
  731.9 30.1 %copy.346 = bf16[2048,2,1,384]{3,1,2,0:T(2,128)(2,1)S(1)} copy(bf16[2048,2,1,384]{3,0,2,1:T(8,128)(2,1)S(1)} %pad_maximum_fusion.1) | data formatting | bytes 6291456 | tf_op jit(solution)/shard_map/stack | solution.py:264
  762.0 6.5 all_to_all.39
  768.8 4.9 copy.348
  773.7 8.0 reshape.584
  781.8 6.7 convolution_bitcast_fusion
  788.5 8.3 copy.353
  800.5 3.9 fusion.131
  809.5 5.4 copy.351
  817.9 6.3 copy.350
  828.6 3.2 pad_maximum_fusion
  833.7 7.0 convolution_bitcast_fusion.4
  840.8 33.2 %reduce-scatter.7.cloned.1.call-done = f32[48,384]{1,0:T(8,128)} async-done(((f32[768,384]{1,0:T(8,128)}), f32[48,384]{1,0:T(8,128)}) %reduce-scatter.7.cloned.1.call-update) | async-done | bytes 73744 | tf_op jit(solution)/shard_map/reduce_scatter | solution.py:312
  875.4 148.8 %all-reduce.21.cloned.1.call-done = f32[2,768,768]{2,0,1:T(2,128)} async-done(((f32[2,768,768]{2,0,1:T(2,128)}), f32[2,768,768]{2,0,1:T(2,128)}) %all-reduce.21.cloned.1.call-update) | async-done | bytes 4718608
  1029.0 120.3 %reduce-scatter.13.cloned.1.call-done = f32[48,3]{1,0:T(8,128)} async-done(((f32[768,3]{1,0:T(8,128)}), f32[48,3]{1,0:T(8,128)}) %reduce-scatter.13.cloned.1.call-update) | async-done | bytes 592
  1151.4 133.3 %reduce-scatter.11.cloned.1.call-done = f32[1024,48]{0,1:T(8,128)} async-done(((f32[1024,768]{0,1:T(8,128)}), f32[1024,48]{0,1:T(8,128)}) %reduce-scatter.11.cloned.1.call-update) | async-done | bytes 196624 | tf_op jit(solution)/shard_map/reduce_scatter | solution.py:315
  1286.3 232.5 %all-reduce.23.cloned.1.call-done = (f32[3,768,384]{2,0,1:T(4,128)}, f32[2,384,768]{1,0,2:T(2,128)}) async-done(((f32[3,768,384]{2,0,1:T(4,128)}, f32[2,384,768]{1,0,2:T(2,128)}), (f32[3,768,384]{2,0,1:T(4,128)}, f32[2,384,768]{1,0,2:T(2,128)})) %all-reduce.23.cloned.1.call-update) | async-done | bytes 5898256
  1524.1 145.2 %reduce-scatter.9.cloned.1.call-done = f32[2,48,1024]{2,1,0:T(8,128)} async-done(((f32[2,768,1024]{2,1,0:T(8,128)}), f32[2,48,1024]{2,1,0:T(8,128)}) %reduce-scatter.9.cloned.1.call-update) | async-done | bytes 393232 | tf_op jit(solution)/shard_map/reduce_scatter | solution.py:314
  1675.5 39.7 %psum.55 = f32[]{:T(128)} all-reduce(f32[]{:T(128)S(6)} %add.425), channel_id=1, replica_groups=mesh['dp'=16,'head'=2] {'dp','head'}, use_global_device_ids=true, to_apply=%region_47.48 | all-reduce | flops 1 | bytes 8 | tf_op jit(solution)/shard_map/psum | solution.py:332
  (530 shorter events, 413.0 us)
Async XLA Ops:
  8.0 197.2 %copy-start = (bf16[1024,768]{1,0:T(8,128)(2,1)S(1)}, bf16[1024,768]{1,0:T(8,128)(2,1)}, u32[]{:S(2)}) copy-start(bf16[1024,768]{1,0:T(8,128)(2,1)} %param.47) | copy-start | bytes 4718596
  8.0 65.9 %copy-start.2 = (bf16[512,768]{1,0:T(8,128)(2,1)S(1)}, bf16[512,768]{1,0:T(8,128)(2,1)}, u32[]{:S(2)}) copy-start(bf16[512,768]{1,0:T(8,128)(2,1)} %param.46) | copy-start | bytes 2359300
  8.1 49.4 %copy-start.74 = (s32[2]{0:T(128)S(1)}, s32[2]{0:T(128)}, u32[]{:S(2)}) copy-start(s32[2]{0:T(128)} %param.52) | copy-start | bytes 28
  8.1 65.9 %all-gather.7.cloned.1.call-start = ((), (), s32[]{:S(2)}) async-start(), calls=%async_computation.6 | async-start | bytes 1880064 | tf_op jit(solution)/shard_map/all_gather | solution.py:183
  9.9 131.2 %all-gather.9.cloned.1.call-start = ((), (), s32[]{:S(2)}) async-start(), calls=%async_computation.7 | async-start | bytes 1253376 | tf_op jit(solution)/shard_map/all_gather | solution.py:185
  11.5 179.3 %all-reduce.13.cloned.1.call-start = ((), (), s32[]{:S(2)}) async-start(), calls=%async_computation.8 | async-start | bytes 1572864 | tf_op jit(solution)/shard_map/psum | solution.py:32
  55.4 21.2 %copy-start.56 = (f32[768]{0:T(1024)}, f32[768]{0:T(1024)S(1)}, u32[]{:S(2)}) copy-start(f32[768]{0:T(1024)S(1)} %get-tuple-element.1214) | copy-start | bytes 9220
  55.5 137.0 %copy-start.52 = (f32[768]{0:T(1024)}, f32[768]{0:T(1024)S(1)}, u32[]{:S(2)}) copy-start(f32[768]{0:T(1024)S(1)} %get-tuple-element.1213) | copy-start | bytes 9220
  57.4 19.3 %copy-start.60 = (f32[512]{0:T(512)}, f32[512]{0:T(512)S(1)}, u32[]{:S(2)}) copy-start(f32[512]{0:T(512)S(1)} %fusion.116) | copy-start | bytes 6148
  141.1 49.7 %copy-start.13 = (bf16[2,256,384]{2,1,0:T(8,128)(2,1)}, bf16[2,256,384]{2,1,0:T(8,128)(2,1)S(1)}, u32[]{:S(2)}) copy-start(bf16[2,256,384]{2,1,0:T(8,128)(2,1)S(1)} %copy.334) | copy-start | bytes 1179652
  141.1 4.2 copy-start.67
  143.8 61.4 %all-gather.11.cloned.1.call-start = ((), (), s32[]{:S(2)}) async-start(), calls=%async_computation.9 | async-start | bytes 2433024 | tf_op jit(solution)/shard_map/all_gather | solution.py:190
  144.6 157.1 %all-reduce.15.cloned.1.call-start = ((), (), s32[]{:S(2)}) async-start(), calls=%async_computation.10 | async-start | bytes 1572864 | tf_op jit(solution)/shard_map/psum | solution.py:32
  280.7 4.5 copy-start.15
  283.5 90.7 %all-gather.13.cloned.1.call-start = ((), (), s32[]{:S(2)}) async-start(), calls=%async_computation.11 | async-start | bytes 3342336 | tf_op jit(solution)/shard_map/all_gather | solution.py:186
  285.3 148.5 %all-gather.15.cloned.1.call-start = ((), (), s32[]{:S(2)}) async-start(), calls=%async_computation.12 | async-start | bytes 1671168 | tf_op jit(solution)/shard_map/all_gather | solution.py:187
  286.9 174.7 %all-reduce.17.cloned.1.call-start = ((), (), s32[]{:S(2)}) async-start(), calls=%async_computation.13 | async-start | bytes 1572864 | tf_op jit(solution)/shard_map/psum | solution.py:32
  374.2 4.1 copy-start.29
  374.2 4.1 copy-start.72
  433.8 6.4 copy-start.73
  443.5 120.6 %all-reduce.19.cloned.1.call-start = ((), (), s32[]{:S(2)}) async-start(), calls=%async_computation.14 | async-start | bytes 1572864 | tf_op jit(solution)/shard_map/psum | solution.py:32
  543.5 253.4 %all-reduce.25.cloned.1.call-start = ((), (), s32[]{:S(2)}) async-start(), calls=%async_computation.21 | async-start | bytes 3145728 | tf_op jit(solution)/shard_map/psum | solution.py:32
  543.7 20.3 %copy-start.53 = (f32[768]{0:T(1024)S(1)}, f32[768]{0:T(1024)}, u32[]{:S(2)}) copy-start(f32[768]{0:T(1024)} %copy-done.52) | copy-start | bytes 9220
  543.7 20.3 %copy-start.59 = (f32[512]{0:T(512)S(1)}, f32[512]{0:T(512)}, u32[]{:S(2)}) copy-start(f32[512]{0:T(512)} %copy-done.58) | copy-start | bytes 6148
  547.4 18.7 %copy-start.65 = (f32[512]{0:T(512)S(1)}, f32[512]{0:T(512)}, u32[]{:S(2)}) copy-start(f32[512]{0:T(512)} %copy-done.64) | copy-start | bytes 6148
  721.2 152.8 %reduce-scatter.7.cloned.1.call-start = ((), (), s32[]{:S(2)}) async-start(), calls=%async_computation.15 | async-start | bytes 1253376 | tf_op jit(solution)/shard_map/reduce_scatter | solution.py:312
  724.2 300.1 %all-reduce.21.cloned.1.call-start = ((), (), s32[]{:S(2)}) async-start(), calls=%async_computation.19 | async-start | bytes 9437184
  796.8 3.7 copy-start.20
  796.8 352.5 %reduce-scatter.13.cloned.1.call-start = ((), (), s32[]{:S(2)}) async-start(), calls=%async_computation.18 | async-start | bytes 417792
  800.4 484.3 %reduce-scatter.11.cloned.1.call-start = ((), (), s32[]{:S(2)}) async-start(), calls=%async_computation.17 | async-start | bytes 3342336 | tf_op jit(solution)/shard_map/reduce_scatter | solution.py:315
  804.4 714.3 %all-reduce.23.cloned.1.call-start = ((), (), s32[]{:S(2)}) async-start(), calls=%async_computation.20 | async-start | bytes 14155776
  809.5 5.4 copy-start.36
  809.5 5.4 copy-start.38
  809.5 5.4 copy-start.39
  824.2 845.1 %reduce-scatter.9.cloned.1.call-start = ((), (), s32[]{:S(2)}) async-start(), calls=%async_computation.16 | async-start | bytes 6684672 | tf_op jit(solution)/shard_map/reduce_scatter | solution.py:314
  833.7 192.2 %copy-start.63 = (f32[512]{0:T(512)S(1)}, f32[512]{0:T(512)}, u32[]{:S(2)}) copy-start(f32[512]{0:T(512)} %copy-done.62) | copy-start | bytes 6148
  833.7 192.2 %copy-start.21 = (bf16[512,768]{1,0:T(8,128)(2,1)S(1)}, bf16[512,768]{1,0:T(8,128)(2,1)}, u32[]{:S(2)}) copy-start(bf16[512,768]{1,0:T(8,128)(2,1)} %get-tuple-element.1298) | copy-start | bytes 2359300
  1029.0 643.9 %copy-start.31 = (bf16[512,768]{1,0:T(8,128)(2,1)S(1)}, bf16[512,768]{1,0:T(8,128)(2,1)}, u32[]{:S(2)}) copy-start(bf16[512,768]{1,0:T(8,128)(2,1)} %get-tuple-element.1297) | copy-start | bytes 2359300
  1672.9 43.0 %copy-start.68 = (f32[3,48]{1,0:T(4,128)S(1)}, f32[3,48]{1,0:T(4,128)}, u32[]{:S(2)}) copy-start(f32[3,48]{1,0:T(4,128)} %param.53) | copy-start | bytes 1732
  1672.9 43.0 %copy-start.69 = (f32[3,48]{1,0:T(4,128)S(1)}, f32[3,48]{1,0:T(4,128)}, u32[]{:S(2)}) copy-start(f32[3,48]{1,0:T(4,128)} %param.54) | copy-start | bytes 1732
  1672.9 43.0 %copy-start.70 = (f32[3,48]{1,0:T(4,128)S(1)}, f32[3,48]{1,0:T(4,128)}, u32[]{:S(2)}) copy-start(f32[3,48]{1,0:T(4,128)} %param.55) | copy-start | bytes 1732
  1672.9 43.6 %copy-start.32 = (f32[2,384,48]{1,2,0:T(8,128)S(1)}, f32[2,384,48]{1,2,0:T(8,128)}, u32[]{:S(2)}) copy-start(f32[2,384,48]{1,2,0:T(8,128)} %param.65) | copy-start | bytes 442372
  1673.0 45.4 %copy-start.34 = (f32[2,24,768]{2,1,0:T(8,128)S(1)}, f32[2,24,768]{2,1,0:T(8,128)}, u32[]{:S(2)}) copy-start(f32[2,24,768]{2,1,0:T(8,128)} %param.62) | copy-start | bytes 442372
  1675.5 44.8 %copy-start.26 = (f32[3,48,384]{2,1,0:T(8,128)S(1)}, f32[3,48,384]{2,1,0:T(8,128)}, u32[]{:S(2)}) copy-start(f32[3,48,384]{2,1,0:T(8,128)} %param.56) | copy-start | bytes 663556
  1718.4 4.0 copy-start.27
  1718.4 4.0 copy-start.28
  1718.4 4.0 copy-start.45
  1718.4 4.0 copy-start.46
  (53 other events, 103.0 us)
Sparse Core Ops, SparseCore 0:
  12.2 61.7 all-gather.6
  77.2 55.1 all-gather.8
  144.0 17.9 all-reduce.12
  283.6 18.0 all-reduce.14
  304.8 69.3 all-gather.12
  377.4 56.3 all-gather.14
  443.6 17.9 all-reduce.16
  543.6 20.3 all-reduce.18
  721.3 21.6 all-reduce.24
  748.3 125.5 reduce-scatter.6
  880.6 143.6 all-reduce.20
  1028.8 120.4 reduce-scatter.12
  1155.1 129.5 reduce-scatter.10
  1292.1 226.5 all-reduce.22
  1524.6 144.5 reduce-scatter.8
Sparse Core Ops, SparseCore 1:
  148.3 56.9 all-gather.10
where the time goes:
time: 1750 us; the launch traced here: 1730 us
  waiting for transfers between devices  1010 us (58%)
  matrix products  275 us (16%)
  local copies, waits for them, and re-layouts  197 us (11%)
  blocking collectives  141 us (8%)
  other arithmetic  83.7 us (5%)
  between operations  23.9 us (1%)
    unnamed x19, waiting for transfers between devices  502 us
    reduce_scatter x1, waiting for transfers between devices, per_device(): lax.psum_scatter(grad_mlp_input, 'dp', scatter_dimension=1, tiled=True)  145 us
    reduce_scatter x1, waiting for transfers between devices, per_device(): lax.psum_scatter(grad_mlp_output, 'dp', scatter_dimension=1, tiled=True)  133 us
    all_gather x1, waiting for transfers between devices, per_device(): lax.all_gather(mlp_input.astype(jnp.bfloat16), 'dp', axis=1, tiled=True)  68.7 us
    all_gather x1, waiting for transfers between devices, per_device(): lax.all_gather(mlp_output.astype(jnp.bfloat16), 'dp', axis=1, tiled=True)  53.2 us
    dot_general x24, matrix products, masked_scores(): jnp.einsum('qd,kd->qk', query_head, key_head, preferred_element_type=jnp....  52.7 us
    psum x5, waiting for transfers between devices, head_total(): lax.psum(partial_value.astype(jnp.bfloat16), 'head').astype(jnp.float32)  49 us
    all_gather x1, blocking collectives, per_device(): lax.all_gather(query_cross.astype(jnp.bfloat16), 'dp', axis=0, tiled=True)  44.9 us
  transfers between devices with their start and end apart: 16, of which 13 were waited for; matrix products, arithmetic and copies ran while one was open for 12% of the time, Pallas kernels for 0%

commit v1 on v0

v1 whole, which is shorter than its diff:
```python
import functools

import jax
import jax.numpy as jnp
from jax import lax
from jax.experimental import pallas as pl
from jax.experimental.pallas import tpu as pltpu
from jax.sharding import PartitionSpec as P

D = 768
HD = 64
FF = 2048
TXT = 256
STEP = 10

BETA1 = 0.9
BETA2 = 0.95
ADAM_EPS = 1e-08
DECAY = 0.1
CLIP = 1.0
NORM_EPS = 1e-06
MASKED = -1e30

MESH = pl.DeviceIdType.MESH
BF = jnp.bfloat16
F32 = jnp.float32
VMEM_BYTES = 63 * 2**20

HALF = D // 2
FT = 256
FH = FF // 2
GAIN = 0
CQ = 128
CKV = CQ + 3 * HALF
COS = CKV + 2 * HALF
CQC = COS + HALF
COC = CQC + HALF
CM = COC + HALF
PACK = CM + 3 * FH


def as_bf(value):
    return value.astype(BF)


def as_f32(value):
    return value.astype(F32)


def nn(left, right):
    return lax.dot_general(left, right, (((1,), (0,)), ((), ())), preferred_element_type=F32)


def nt(left, right):
    return lax.dot_general(left, right, (((1,), (1,)), ((), ())), preferred_element_type=F32)


def tn(left, right):
    return lax.dot_general(left, right, (((0,), (0,)), ((), ())), preferred_element_type=F32)


def bit_count(n):
    return n.bit_length() - 1


def gather_jobs(bits):
    if bits == 4:
        first = ((3, 2, 0, 1), (3, 2, 1, 0))
        later = ((0, 3, 2, 1), (1, 3, 2, 0))
    else:
        plain = tuple(range(bits))
        first = later = (plain, plain[::-1])
    bounds = [0, CKV, COS, CM]
    while bounds[-1] < PACK:
        bounds.append(bounds[-1] + 3 * FT)
    jobs = []
    for number, (low, high) in enumerate(zip(bounds[:-1], bounds[1:])):
        middle = low + (high - low) // 256 * 128
        orders = first if number % 3 == 0 else later
        jobs.append((low, middle, orders[0]))
        jobs.append((middle, high, orders[1]))
    return jobs


def block_index(bits, me, free, fixed=None):
    fixed = fixed or {}
    out = []
    for bit in reversed(range(bits)):
        if bit in free:
            out.append(slice(None))
        elif bit in fixed:
            out.append(fixed[bit])
        else:
            out.append((me >> bit) & 1)
    return tuple(out)


def greet(me, head, bits):
    barrier = pltpu.get_barrier_semaphore()
    for bit in range(bits):
        pl.semaphore_signal(barrier, inc=1, device_id=(me ^ (1 << bit), head), device_id_type=MESH)
    pl.semaphore_signal(barrier, inc=1, device_id=(me, 1 - head), device_id_type=MESH)
    pl.semaphore_wait(barrier, bits + 1)


class Gather:
    def __init__(self, bits, me, head, wall, send_sem, recv_sem):
        self.bits, self.me, self.head = bits, me, head
        self.wall, self.send_sem, self.recv_sem = wall, send_sem, recv_sem
        self.jobs = gather_jobs(bits)

    def copy(self, number, phase, received=False):
        low, high, order = self.jobs[number]
        bit = order[phase]
        mine = (self.me >> bit) & 1
        fixed = {bit: 1 - mine if received else mine}
        index = block_index(self.bits, self.me, order[:phase], fixed)
        ref = self.wall.at[index + (slice(None), slice(low, high))]
        return pltpu.make_async_remote_copy(
            src_ref=ref,
            dst_ref=ref,
            send_sem=self.send_sem.at[number, phase],
            recv_sem=self.recv_sem.at[number, phase],
            device_id=(self.me ^ (1 << bit), self.head),
            device_id_type=MESH,
        )

    def start(self, number, phase):
        self.copy(number, phase).start()

    def wait(self, number, phase):
        self.copy(number, phase, True).wait_recv()

    def finish(self):
        for number in range(len(self.jobs)):
            for phase in range(self.bits):
                self.copy(number, phase).wait_send()


def gather_kernel(bits, pack_ref, mem_ref, wall_ref, memall_ref, send_sem, recv_sem, local_sem, mem_sem):
    me, head = lax.axis_index("dp"), lax.axis_index("head")
    greet(me, head, bits)
    own = pltpu.make_async_copy(
        pack_ref, wall_ref.at[block_index(bits, me, ())], local_sem.at[0]
    )
    own.start()
    mem_copy = pltpu.make_async_remote_copy(
        src_ref=mem_ref,
        dst_ref=memall_ref.at[head],
        send_sem=mem_sem.at[0],
        recv_sem=mem_sem.at[1],
        device_id=(me, 1 - head),
        device_id_type=MESH,
    )
    mem_copy.start()
    mem_local = pltpu.make_async_copy(mem_ref, memall_ref.at[head], local_sem.at[1])
    mem_local.start()
    own.wait()
    gather = Gather(bits, me, head, wall_ref, send_sem, recv_sem)
    count = len(gather.jobs)
    groups = count // 2
    for turn in range(groups + bits):
        for group in range(groups):
            phase = turn - group
            for number in (2 * group, 2 * group + 1):
                if 1 <= phase <= bits:
                    gather.wait(number, phase - 1)
                if 0 <= phase < bits:
                    gather.start(number, phase)
    gather.finish()
    mem_local.wait()
    mem_copy.wait_send()
    pltpu.make_async_remote_copy(
        src_ref=mem_ref,
        dst_ref=memall_ref.at[1 - head],
        send_sem=mem_sem.at[0],
        recv_sem=mem_sem.at[1],
        device_id=(me, 1 - head),
        device_id_type=MESH,
    ).wait_recv()


def gather_weights(pack, memory, count):
    bits = bit_count(count)
    rows = pack.shape[0]
    jobs = len(gather_jobs(bits))
    wall, memall = pl.pallas_call(
        functools.partial(gather_kernel, bits),
        out_shape=(
            jax.ShapeDtypeStruct((2,) * bits + (rows, PACK), BF),
            jax.ShapeDtypeStruct((2,) + memory.shape, BF),
        ),
        in_specs=[pl.BlockSpec(memory_space=pl.ANY)] * 2,
        out_specs=(pl.BlockSpec(memory_space=pl.ANY),) * 2,
        scratch_shapes=[
            pltpu.SemaphoreType.DMA((jobs, bits)),
            pltpu.SemaphoreType.DMA((jobs, bits)),
            pltpu.SemaphoreType.DMA((2,)),
            pltpu.SemaphoreType.DMA((2,)),
        ],
        name="gather",
        compiler_params=pltpu.CompilerParams(
            collective_id=1, has_side_effects=True, vmem_limit_bytes=VMEM_BYTES
        ),
    )(pack, memory)
    return wall.reshape(count * rows, PACK), memall.reshape(2 * memory.shape[0], D)


class Exchange:
    def __init__(self, me, head, send, recv, send_sem, recv_sem):
        self.me, self.head = me, head
        self.send, self.recv, self.send_sem, self.recv_sem = send, recv, send_sem, recv_sem

    def copy(self, number):
        slot = number % 2
        return pltpu.make_async_remote_copy(
            src_ref=self.send.at[slot],
            dst_ref=self.recv.at[slot],
            send_sem=self.send_sem.at[number],
            recv_sem=self.recv_sem.at[number],
            device_id=(self.me, 1 - self.head),
            device_id_type=MESH,
        )

    def start(self, number, value):
        self.send[number % 2] = as_bf(value)
        self.copy(number).start()

    def wait(self, number):
        self.copy(number).wait()

    def total(self, number, rows=slice(None)):
        slot = number % 2
        return as_f32(self.send[slot, rows]) + as_f32(self.recv[slot, rows])


def inverse_rms(values):
    return lax.rsqrt(jnp.mean(values * values, axis=-1, keepdims=True) + NORM_EPS)


def norm_back(values, gain, grad):
    inverse = inverse_rms(values)
    scaled = grad * gain
    inner = jnp.mean(scaled * values, axis=-1, keepdims=True)
    grad_values = inverse * scaled - values * (inverse * inverse * inverse * inner)
    grad_gain = jnp.sum(grad * values * inverse, axis=0, keepdims=True)
    return grad_values, grad_gain


def layer_kernel(
    tok, mem, cot, cbias, sbias, wall,
    out, tgrad, mgrad, dwall,
    ws, gains, dgains, n1, n2, n3, x1, x2, q3, k3, v3, o3, oT, qc3, oc3, ocT,
    kext, mv3, mT, exps, sexps, linv, slinv, st, acc, do3, dqc3, dT4, q4,
    esend, erecv, osend, orecv, msend, mrecv,
    send_sem, recv_sem, side_sem, wsem, msem,
):
    me, head = lax.axis_index("dp"), lax.axis_index("head")
    load = pltpu.make_async_copy(wall, ws, wsem.at[0])
    load.start()
    barrier = pltpu.get_barrier_semaphore()
    pl.semaphore_signal(barrier, inc=1, device_id=(me, 1 - head), device_id_type=MESH)
    pl.semaphore_wait(barrier, 1)
    load.wait()
    ex = Exchange(me, head, esend, erecv, send_sem, recv_sem)

    def w(column, width):
        return ws[:, pl.ds(column, width)]

    patches = mem.shape[0]
    lane = lax.broadcasted_iota(jnp.int32, (TXT, 128), 1)
    mask = [as_bf(jnp.where(lane < HD, 1.0, 0.0)), as_bf(jnp.where(lane < HD, 0.0, 1.0))]
    texts = [slice(0, TXT), slice(TXT, 2 * TXT)]
    pairs = 3

    gains[...] = as_f32(ws[:, 0:128]).T[0:8]
    dgains[...] = jnp.zeros_like(dgains)

    for rows in texts:
        x = as_f32(tok[rows])
        n1[rows] = as_bf(x * inverse_rms(x) * gains[0:1])
    for number, target in enumerate((q3, k3, v3)):
        value = as_bf(nn(n1[...], w(CQ + number * HALF, HALF)))
        if number == 0:
            value = value * jnp.asarray(HD**-0.5, BF)
        for j in range(pairs):
            target[j] = value[:, j * 128 : (j + 1) * 128]

    def softmax_parts(scores):
        top = jnp.max(scores, axis=0, keepdims=True)
        expo = jnp.exp(scores - top)
        return expo, jnp.sum(expo, axis=0, keepdims=True)

    def self_forward(j, carry):
        for t in range(2):
            query, key = q3[j, texts[t]], k3[j, texts[t]]
            turned = v3[j, texts[t]].T
            parts = []
            for a in range(2):
                scores = nt(key, query * mask[a]) + as_f32(sbias[t])
                expo, total = softmax_parts(scores)
                low = as_bf(expo)
                sexps[j, t, a] = low
                inverse = 1.0 / total
                slinv[j, t, a] = jnp.broadcast_to(inverse, (8, TXT))
                parts.append(nn(turned[a * HD : (a + 1) * HD], low) * inverse)
            both = jnp.concatenate(parts, axis=0)
            oT[j, t] = as_bf(both)
            o3[j, texts[t]] = as_bf(both.T)
        return carry

    lax.fori_loop(0, pairs, self_forward, 0)

    def joined(ref, rows=slice(None)):
        return jnp.concatenate([ref[j, rows] for j in range(pairs)], axis=1)

    ex.start(0, nt(joined(o3), w(COS, HALF)))

    def project(c, carry):
        rows = pl.ds(pl.multiple_of(c * 512, 512), 512)
        both = as_bf(nn(mem[rows], w(CKV, 2 * HALF)))
        for j in range(pairs):
            kext[j, rows, 0:128] = both[:, j * 128 : (j + 1) * 128]
            kext[j, rows, 128:256] = cbias[rows]
            mv3[j, rows] = both[:, HALF + j * 128 : HALF + (j + 1) * 128]
        return carry

    lax.fori_loop(0, patches // 512, project, 0)
    for j in range(pairs):
        mT[j] = mv3[j].T

    ex.wait(0)
    for rows in texts:
        value = as_f32(tok[rows]) + ex.total(0, rows)
        x1[rows] = value
        n2[rows] = as_bf(value * inverse_rms(value) * gains[1:2])
    value = as_bf(nn(n2[...], w(CQC, HALF))) * jnp.asarray(HD**-0.5, BF)
    for j in range(pairs):
        qc3[j] = value[:, j * 128 : (j + 1) * 128]

    def cross_forward(jt, carry):
        j, t = jt // 2, jt % 2
        rows = pl.ds(pl.multiple_of(t * TXT, TXT), TXT)
        query = qc3[j, rows]
        pick = as_bf(jnp.where(lane == t, 1.0, 0.0))
        parts = []
        for a in range(2):
            wide = jnp.concatenate([query * mask[a], pick], axis=1)
            top = jnp.full((8, TXT), -3e38, F32)
            for c in range(patches // 256):
                scores = nt(kext[j, c * 256 : (c + 1) * 256], wide)
                st[c * 256 : (c + 1) * 256] = scores
                top = jnp.maximum(top, jnp.max(scores.reshape(32, 8, TXT), axis=0))
            top = jnp.max(top, axis=0, keepdims=True)
            total = jnp.zeros((8, TXT), F32)
            for c in range(patches // 128):
                expo = jnp.exp(st[c * 128 : (c + 1) * 128] - top)
                total = total + jnp.sum(expo.reshape(16, 8, TXT), axis=0)
                exps[jt, a, c * 128 : (c + 1) * 128] = as_bf(expo)
            inverse = 1.0 / jnp.sum(total, axis=0, keepdims=True)
            linv[jt, a] = jnp.broadcast_to(inverse, (8, TXT))
            parts.append(nn(mT[j, a * HD : (a + 1) * HD], exps[jt, a]) * inverse)
        both = jnp.concatenate(parts, axis=0)
        ocT[jt] = as_bf(both)
        oc3[j, rows] = as_bf(both.T)
        return carry

    lax.fori_loop(0, 2 * pairs, cross_forward, 0)
    ex.start(1, nt(joined(oc3), w(COC, HALF)))
    for j in range(pairs):
        mT[j] = kext[j, :, 0:128].T
    ex.wait(1)
    for rows in texts:
        value = x1[rows] + ex.total(1, rows)
        x2[rows] = value
        n3[rows] = as_bf(value * inverse_rms(value) * gains[2:3])

    acc[...] = jnp.zeros_like(acc)
    tgrad[...] = jnp.zeros_like(tgrad)
    root = (2.0 / jnp.pi) ** 0.5

    def mlp(f, carry):
        base = pl.multiple_of(CM + f * (3 * FT), 128)
        gate_w, up_w, down_w = (ws[:, pl.ds(base + k * FT, FT)] for k in range(3))
        for rows in texts:
            gate, up = nn(n3[rows], gate_w), nn(n3[rows], up_w)
            grad = nn(cot[rows], down_w)
            square = gate * gate
            tanh = jnp.tanh(root * gate * (1.0 + 0.044715 * square))
            half = 0.5 * (1.0 + tanh)
            slope = half + 0.5 * gate * (1.0 - tanh * tanh) * (root * (1.0 + 3 * 0.044715 * square))
            active = gate * half
            osend[rows, 0:FT] = as_bf(active * up)
            osend[rows, FT : 2 * FT] = as_bf(grad * up * slope)
            osend[rows, 2 * FT : 3 * FT] = as_bf(grad * active)
        for rows in texts:
            acc[rows] += nt(osend[rows, 0:FT], down_w)
            tgrad[rows] += nt(osend[rows, FT : 2 * FT], gate_w) + nt(osend[rows, 2 * FT : 3 * FT], up_w)
        ws[:, pl.ds(base, FT)] = as_bf(tn(n3[...], osend[:, FT : 2 * FT]))
        ws[:, pl.ds(base + FT, FT)] = as_bf(tn(n3[...], osend[:, 2 * FT : 3 * FT]))
        ws[:, pl.ds(base + 2 * FT, FT)] = as_bf(tn(cot[...], osend[:, 0:FT]))
        return carry

    lax.fori_loop(0, FH // FT, mlp, 0)
    ex.start(2, tgrad[...])
    osend[...] = as_bf(acc[...])
    side = pltpu.make_async_remote_copy(
        src_ref=osend, dst_ref=orecv, send_sem=side_sem.at[0], recv_sem=side_sem.at[1],
        device_id=(me, 1 - head), device_id_type=MESH,
    )
    side.start()
    ex.wait(2)
    side.wait()
    for rows in texts:
        out[rows] = as_bf(x2[rows] + (as_f32(osend[rows]) + as_f32(orecv[rows])))
        grad, grad_gain = norm_back(x2[rows], gains[2:3], ex.total(2, rows))
        value = as_f32(cot[rows]) + grad
        x2[rows] = value
        dgains[2:3] += grad_gain
        back = as_bf(value)
        n3[rows] = back
        turned = as_bf(nn(back, w(COC, HALF)))
        for j in range(pairs):
            do3[j, rows] = turned[:, j * 128 : (j + 1) * 128]

    def split_grad(grad, attended, inverse, a):
        part = grad[a * HD : (a + 1) * HD] * inverse
        low = as_bf(part)
        inner = jnp.sum(as_f32(low) * attended[a * HD : (a + 1) * HD], axis=0, keepdims=True)
        empty = jnp.zeros_like(low)
        return jnp.concatenate([low, empty] if a == 0 else [empty, low], axis=0), inner

    def cross_back(j, carry):
        def one_text(t, inner_carry):
            jt = 2 * j + t
            rows = pl.ds(pl.multiple_of(t * TXT, TXT), TXT)
            grad = as_f32(do3[j, rows]).T
            attended = as_f32(ocT[jt])
            query = qc3[j, rows]
            parts = []
            for a in range(2):
                low, inner = split_grad(grad, attended, linv[jt, a, 0:1], a)
                dT4[2 * t + a] = low
                q4[2 * t + a] = query * mask[a]
            return inner_carry

        lax.fori_loop(0, 2, one_text, 0)
        turned = [dT4[i] for i in range(4)]
        for c in range(patches // 512):
            rows = slice(c * 512, (c + 1) * 512)
            total = nt(exps[2 * j, 0, rows], turned[0])
            for i in range(1, 4):
                total = total + nt(exps[2 * j + i // 2, i % 2, rows], turned[i])
            st[rows, 0:128] = total

        def back_text(t, inner_carry):
            jt = 2 * j + t
            rows = pl.ds(pl.multiple_of(t * TXT, TXT), TXT)
            attended = as_f32(ocT[jt])
            parts = []
            for a in range(2):
                low = dT4[2 * t + a]
                inner = jnp.sum(
                    as_f32(low[a * HD : (a + 1) * HD]) * attended[a * HD : (a + 1) * HD], axis=0, keepdims=True
                )
                for c in range(patches // 128):
                    keys = slice(c * 128, (c + 1) * 128)
                    grad_probs = nn(mv3[j, keys], low)
                    exps[jt, a, keys] = as_bf(as_f32(exps[jt, a, keys]) * (grad_probs - inner))
                parts.append(nn(mT[j, a * HD : (a + 1) * HD], exps[jt, a]))
            dqc3[j, rows] = as_bf((jnp.concatenate(parts, axis=0) * HD**-0.5).T)
            return inner_carry

        lax.fori_loop(0, 2, back_text, 0)
        queries = [q4[i] for i in range(4)]
        for c in range(patches // 512):
            rows = slice(c * 512, (c + 1) * 512)
            mv3[j, rows] = as_bf(st[rows, 0:128])
            total = nn(exps[2 * j, 0, rows], queries[0])
            for i in range(1, 4):
                total = total + nn(exps[2 * j + i // 2, i % 2, rows], queries[i])
            kext[j, rows, 0:128] = as_bf(total)
        return carry

    lax.fori_loop(0, pairs, cross_back, 0)
    ex.start(3, nt(joined(dqc3), w(CQC, HALF)))

    half_rows = patches // 2

    def memory_back(c, start):
        rows = pl.ds(pl.multiple_of(start + c * 256, 256), 256)
        both = jnp.concatenate(
            [kext[j, rows, 0:128] for j in range(pairs)] + [mv3[j, rows] for j in range(pairs)], axis=1
        )
        return nt(both, w(CKV, 2 * HALF))

    def send_part(c, carry):
        msend[pl.ds(pl.multiple_of(c * 256, 256), 256)] = as_bf(memory_back(c, (1 - head) * half_rows))
        return carry

    lax.fori_loop(0, half_rows // 256, send_part, 0)
    mside = pltpu.make_async_remote_copy(
        src_ref=msend, dst_ref=mrecv, send_sem=side_sem.at[2], recv_sem=side_sem.at[3],
        device_id=(me, 1 - head), device_id_type=MESH,
    )
    mside.start()
    ws[:, COC : COC + HALF] = as_bf(tn(n3[...], joined(oc3)))
    ws_query = as_bf(tn(n2[...], joined(dqc3)))
    mside.wait()
    stores = []
    for c in range(half_rows // 256):
        if c >= 2:
            stores[c - 2].wait()
        slot = slice((c % 2) * 256, (c % 2 + 1) * 256)
        acc[slot] = memory_back(c, head * half_rows) + as_f32(mrecv[c * 256 : (c + 1) * 256])
        store = pltpu.make_async_copy(acc.at[slot], mgrad.at[pl.ds(c * 256, 256)], msem.at[c])
        store.start()
        stores.append(store)
    for number in range(2):
        total = jnp.zeros((D, HALF), F32)
        source = kext if number == 0 else mv3
        for c in range(patches // 512):
            rows = slice(c * 512, (c + 1) * 512)
            both = jnp.concatenate([source[j, rows, 0:128] for j in range(pairs)], axis=1)
            total = total + tn(mem[rows], both)
        ws[:, CKV + number * HALF : CKV + (number + 1) * HALF] = as_bf(total)
    ex.wait(3)
    ws[:, CQC : CQC + HALF] = ws_query
    for rows in texts:
        grad, grad_gain = norm_back(x1[rows], gains[1:2], ex.total(3, rows))
        value = x2[rows] + grad
        x1[rows] = value
        dgains[1:2] += grad_gain
        back = as_bf(value)
        n3[rows] = back
        turned = as_bf(nn(back, w(COS, HALF)))
        for j in range(pairs):
            do3[j, rows] = turned[:, j * 128 : (j + 1) * 128]

    def self_back(j, carry):
        for t in range(2):
            rows = texts[t]
            grad = as_f32(do3[j, rows]).T
            attended = as_f32(oT[j, t])
            query, key, value = q3[j, rows], k3[j, rows], v3[j, rows]
            key_turned = key.T
            parts = []
            grad_key = jnp.zeros((TXT, 128), F32)
            grad_value = jnp.zeros((TXT, 128), F32)
            for a in range(2):
                low, inner = split_grad(grad, attended, slinv[j, t, a, 0:1], a)
                expo = sexps[j, t, a]
                grad_scores = as_bf(as_f32(expo) * (nn(value, low) - inner))
                grad_value = grad_value + nt(expo, low)
                grad_key = grad_key + nn(grad_scores, query * mask[a])
                parts.append(nn(key_turned[a * HD : (a + 1) * HD], grad_scores))
            q3[j, rows] = as_bf((jnp.concatenate(parts, axis=0) * HD**-0.5).T)
            k3[j, rows] = as_bf(grad_key)
            v3[j, rows] = as_bf(grad_value)
        return carry

    lax.fori_loop(0, pairs, self_back, 0)
    ex.start(
        4,
        nt(joined(q3), w(CQ, HALF)) + nt(joined(k3), w(CQ + HALF, HALF)) + nt(joined(v3), w(CQ + 2 * HALF, HALF)),
    )
    ws[:, COS : COS + HALF] = as_bf(tn(n3[...], joined(o3)))
    for number, source in enumerate((q3, k3, v3)):
        column = CQ + number * HALF
        ws[:, column : column + HALF] = as_bf(tn(n1[...], joined(source)))
    ex.wait(4)
    for rows in texts:
        grad, grad_gain = norm_back(as_f32(tok[rows]), gains[0:1], ex.total(4, rows))
        tgrad[rows] = x1[rows] + grad
        dgains[0:1] += grad_gain
    ws[:, 0:128] = as_bf(dgains[...].T)
    store = pltpu.make_async_copy(ws, dwall, wsem.at[1])
    store.start()
    for number in (-2, -1):
        stores[number].wait()
    store.wait()


def layer(tokens, memory, cotangent, cbias, sbias, wall):
    rows, patches = tokens.shape[0], memory.shape[0]
    vm = pl.BlockSpec(memory_space=pltpu.VMEM)
    anywhere = pl.BlockSpec(memory_space=pl.ANY)
    S = pltpu.VMEM
    scratch = [
        S((D, PACK), BF), S((8, D), F32), S((128, D), F32),
        S((rows, D), BF), S((rows, D), BF), S((rows, D), BF),
        S((rows, D), F32), S((rows, D), F32),
        S((3, rows, 128), BF), S((3, rows, 128), BF), S((3, rows, 128), BF), S((3, rows, 128), BF),
        S((3, 2, 128, TXT), BF), S((3, rows, 128), BF), S((3, rows, 128), BF), S((6, 128, TXT), BF),
        S((3, patches, 256), BF), S((3, patches, 128), BF), S((3, 128, patches), BF),
        S((6, 2, patches, TXT), BF), S((3, 2, 2, TXT, TXT), BF),
        S((6, 2, 8, TXT), F32), S((3, 2, 2, 8, TXT), F32),
        S((patches, TXT), F32),
        S((rows, D), F32),
        S((3, rows, 128), BF), S((3, rows, 128), BF), S((4, 128, TXT), BF), S((4, TXT, 128), BF),
        S((2, rows, D), BF), S((2, rows, D), BF), S((rows, D), BF), S((rows, D), BF),
        S((patches // 2, D), BF), S((patches // 2, D), BF),
        pltpu.SemaphoreType.DMA((5,)), pltpu.SemaphoreType.DMA((5,)), pltpu.SemaphoreType.DMA((4,)),
        pltpu.SemaphoreType.DMA((2,)), pltpu.SemaphoreType.DMA((patches // 512,)),
    ]
    return pl.pallas_call(
        layer_kernel,
        out_shape=(
            jax.ShapeDtypeStruct((rows, D), BF),
            jax.ShapeDtypeStruct((rows, D), F32),
            jax.ShapeDtypeStruct((patches // 2, D), F32),
            jax.ShapeDtypeStruct((D, PACK), BF),
        ),
        in_specs=[vm] * 5 + [anywhere],
        out_specs=(vm, vm, anywhere, anywhere),
        scratch_shapes=scratch,
        name="layer",
        compiler_params=pltpu.CompilerParams(
            collective_id=2, has_side_effects=True, vmem_limit_bytes=VMEM_BYTES
        ),
    )(tokens, memory, cotangent, cbias, sbias, wall)


class Scatter:
    def __init__(self, bits, me, head, wall, slots, send_sem, recv_sem):
        self.bits, self.me, self.head = bits, me, head
        self.wall, self.slots = wall, slots
        self.send_sem, self.recv_sem = send_sem, recv_sem
        self.jobs = [(low, high, order[::-1]) for low, high, order in gather_jobs(bits)]

    def copy(self, number, phase):
        low, high, order = self.jobs[number]
        bit = order[phase]
        index = block_index(self.bits, self.me, order[phase + 1 :], {bit: 1 - ((self.me >> bit) & 1)})
        columns = (slice(None), slice(low, high))
        left = self.bits - 1 - phase
        return pltpu.make_async_remote_copy(
            src_ref=self.wall.at[index + columns],
            dst_ref=self.slots[phase].at[(slice(None),) * left + columns],
            send_sem=self.send_sem.at[number, phase],
            recv_sem=self.recv_sem.at[number, phase],
            device_id=(self.me ^ (1 << bit), self.head),
            device_id_type=MESH,
        )

    def start(self, number, phase):
        self.copy(number, phase).start()

    def add(self, number, phase, final=None):
        self.copy(number, phase).wait_recv()
        low, high, order = self.jobs[number]
        left = [bit for bit in reversed(range(self.bits)) if bit in order[phase + 1 :]]
        for block in range(1 << len(left)):
            fixed = {bit: (block >> (len(left) - 1 - place)) & 1 for place, bit in enumerate(left)}
            here = block_index(self.bits, self.me, (), fixed) + (slice(None), slice(low, high))
            there = tuple(fixed[bit] for bit in left) + (slice(None), slice(low, high))
            if final is None:
                self.wall[here] = self.wall[here] + self.slots[phase][there]
            else:
                final[:, low:high] = as_f32(self.wall[here]) + as_f32(self.slots[phase][there])

    def finish(self):
        for number in range(len(self.jobs)):
            for phase in range(self.bits):
                self.copy(number, phase).wait_send()


def scatter_kernel(bits, dwall, red, total, *rest):
    ws, slots = rest[0], rest[1 : 1 + bits]
    sums, others, send_sem, recv_sem, local_sem, sum_send, sum_recv = rest[1 + bits :]
    me, head = lax.axis_index("dp"), lax.axis_index("head")
    load = pltpu.make_async_copy(dwall, ws, local_sem.at[0])
    load.start()
    greet(me, head, bits)
    load.wait()
    scatter = Scatter(bits, me, head, ws, slots, send_sem, recv_sem)
    groups = len(scatter.jobs) // 2
    for turn in range(groups + bits):
        for place in range(groups):
            group = groups - 1 - place
            phase = turn - place
            for number in (2 * group, 2 * group + 1):
                if 1 <= phase <= bits:
                    scatter.add(number, phase - 1, red if phase == bits else None)
                if 0 <= phase < bits:
                    scatter.start(number, phase)
    first = red[:, 0:128]
    first = jnp.sum(first * first, axis=0, keepdims=True)
    value = jnp.where(head == 0, first, jnp.zeros_like(first))
    for column in range(128, PACK, 128):
        part = red[:, column : column + 128]
        value = value + jnp.sum(part * part, axis=0, keepdims=True)
    value = jnp.broadcast_to(jnp.sum(value, axis=1, keepdims=True), (8, 128))
    for step in range(bits + 1):
        sums[step] = value
        peer = (me, 1 - head) if step == bits else (me ^ (1 << step), head)
        copy = pltpu.make_async_remote_copy(
            src_ref=sums.at[step], dst_ref=others.at[step], send_sem=sum_send.at[step], recv_sem=sum_recv.at[step],
            device_id=peer, device_id_type=MESH,
        )
        copy.start()
        copy.wait()
        value = value + others[step]
    total[...] = value
    scatter.finish()


def scatter_grads(dwall, count):
    bits = bit_count(count)
    rows = D // count
    jobs = len(gather_jobs(bits))
    S = pltpu.VMEM
    vm = pl.BlockSpec(memory_space=pltpu.VMEM)
    red, total = pl.pallas_call(
        functools.partial(scatter_kernel, bits),
        out_shape=(
            jax.ShapeDtypeStruct((rows, PACK), F32),
            jax.ShapeDtypeStruct((8, 128), F32),
        ),
        in_specs=[pl.BlockSpec(memory_space=pl.ANY)],
        out_specs=(vm, vm),
        scratch_shapes=[S((2,) * bits + (rows, PACK), BF)]
        + [S((2,) * (bits - 1 - phase) + (rows, PACK), BF) for phase in range(bits)]
        + [
            S((bits + 1, 8, 128), F32), S((bits + 1, 8, 128), F32),
            pltpu.SemaphoreType.DMA((jobs, bits)), pltpu.SemaphoreType.DMA((jobs, bits)),
            pltpu.SemaphoreType.DMA((1,)),
            pltpu.SemaphoreType.DMA((bits + 1,)), pltpu.SemaphoreType.DMA((bits + 1,)),
        ],
        name="scatter",
        compiler_params=pltpu.CompilerParams(
            collective_id=3, has_side_effects=True, vmem_limit_bytes=VMEM_BYTES
        ),
    )(dwall.reshape((2,) * bits + (rows, PACK)))
    return red, total[0, 0]


def adam_step(weight, first, second, grad, rate, decay):
    first_new = BETA1 * first + (1.0 - BETA1) * grad
    second_new = BETA2 * second + (1.0 - BETA2) * grad * grad
    mean_hat = first_new / (1.0 - BETA1**STEP)
    square_hat = second_new / (1.0 - BETA2**STEP)
    weight_new = weight - rate * (mean_hat / (jnp.sqrt(square_hat) + ADAM_EPS) + decay * weight)
    return (weight_new, first_new, second_new)


def pack_weights(gains, self_proj, query, keyval, out_proj, mlp_input, mlp_output):
    rows = gains.shape[1]
    turned_out = jnp.swapaxes(out_proj, 1, 2)
    turned_down = mlp_output.T
    pieces = [jnp.pad(gains.T, ((0, 0), (0, 125)))]
    pieces += [self_proj[0], self_proj[1], self_proj[2], keyval[0], keyval[1]]
    pieces += [turned_out[0], query, turned_out[1]]
    for tile in range(FH // FT):
        columns = slice(tile * FT, (tile + 1) * FT)
        pieces += [mlp_input[0][:, columns], mlp_input[1][:, columns], turned_down[:, columns]]
    return jnp.concatenate([piece.astype(BF) for piece in pieces], axis=1)


def unpack_grads(red):
    def cut(start, width):
        return red[:, start : start + width]

    gains = cut(GAIN, 3).T
    self_proj = jnp.stack([cut(CQ + i * HALF, HALF) for i in range(3)])
    keyval = jnp.stack([cut(CKV + i * HALF, HALF) for i in range(2)])
    query = cut(CQC, HALF)
    out_proj = jnp.stack([cut(COS, HALF).T, cut(COC, HALF).T])
    tiles = FH // FT
    mlp = [jnp.concatenate([cut(CM + (3 * tile + k) * FT, FT) for tile in range(tiles)], axis=1) for k in range(3)]
    return gains, self_proj, query, keyval, out_proj, jnp.stack(mlp[:2]), mlp[2].T


def per_device(
    tokens, memory, cotangent, patch_item, patch_mask, text_item, text_len,
    norm_gains, gains_mean, gains_square,
    self_proj, self_proj_mean, self_proj_square,
    query_cross, query_cross_mean, query_cross_square,
    keyval_cross, keyval_cross_mean, keyval_cross_square,
    out_proj, out_proj_mean, out_proj_square,
    mlp_input, mlp_input_mean, mlp_input_square,
    mlp_output, mlp_output_mean, mlp_output_square,
):
    count = lax.axis_size("dp")
    rows = D // count
    direct = rows % 16 == 0 and count & (count - 1) == 0
    keyval_own = lax.all_to_all(keyval_cross.astype(BF), "head", split_axis=2, concat_axis=1, tiled=True)
    pack = pack_weights(norm_gains, self_proj, query_cross, keyval_own, out_proj, mlp_input, mlp_output)
    if direct:
        wall, memall = gather_weights(pack, memory, count)
    else:
        wall = lax.all_gather(pack, "dp", axis=0, tiled=True)
        memall = lax.all_gather(memory, "head", axis=0, tiled=True)
    seen = (text_item[None, :] == patch_item[:, None]) & (patch_mask[:, None] == 1)
    cbias = jnp.pad(jnp.where(seen, 0.0, MASKED), ((0, 0), (0, 126))).astype(BF)
    place = jnp.arange(TXT, dtype=jnp.int32)
    allowed = (place[None, :, None] <= place[None, None, :]) & (place[None, :, None] < text_len[:, None, None])
    sbias = jnp.where(allowed, 0.0, MASKED).astype(BF)
    output, tokens_grad, memory_grad, dwall = layer(tokens, memall, cotangent, cbias, sbias, wall)
    if direct:
        red, total = scatter_grads(dwall, count)
    else:
        red = lax.psum_scatter(dwall.astype(F32), "dp", scatter_dimension=0, tiled=True)
        squares = jnp.sum(red[:, 128:] ** 2)
        squares = squares + jnp.where(lax.axis_index("head") == 0, jnp.sum(red[:, :128] ** 2), 0.0)
        total = lax.psum(squares, ("dp", "head"))
    gains_g, self_g, query_g, keyval_g, out_g, input_g, output_g = unpack_grads(red)
    keyval_g = lax.all_to_all(keyval_g, "head", split_axis=1, concat_axis=2, tiled=True)
    grad_norm = jnp.sqrt(total)
    factor = jnp.minimum(1.0, CLIP / (grad_norm + NORM_EPS))
    wide_rate = 2.0 * D ** (-0.5)
    results = [output, tokens_grad, memory_grad, grad_norm]
    for weight, first, second, grad, rate, decay in (
        (norm_gains, gains_mean, gains_square, gains_g, 0.5, 0.0),
        (self_proj, self_proj_mean, self_proj_square, self_g, wide_rate, DECAY),
        (query_cross, query_cross_mean, query_cross_square, query_g, wide_rate, DECAY),
        (keyval_cross, keyval_cross_mean, keyval_cross_square, keyval_g, wide_rate, DECAY),
        (out_proj, out_proj_mean, out_proj_square, out_g, 2.0 * (D // 16) ** (-0.5), DECAY),
        (mlp_input, mlp_input_mean, mlp_input_square, input_g, wide_rate, DECAY),
        (mlp_output, mlp_output_mean, mlp_output_square, output_g, 2.0 * FF ** (-0.5), DECAY),
    ):
        results += adam_step(weight, first, second, grad * factor, rate, decay)
    return tuple(results)


def solution(mesh):
    in_specs = (
        P("dp", None),
        P(("dp", "head"), None),
        P("dp", None),
        P("dp"),
        P("dp"),
        P("dp"),
        P("dp"),
        P(None, "dp"),
        P(None, "dp"),
        P(None, "dp"),
        P(None, "dp", "head"),
        P(None, "dp", "head"),
        P(None, "dp", "head"),
        P("dp", "head"),
        P("dp", "head"),
        P("dp", "head"),
        P(None, ("dp", "head"), None),
        P(None, ("dp", "head"), None),
        P(None, ("dp", "head"), None),
        P(None, "head", "dp"),
        P(None, "head", "dp"),
        P(None, "head", "dp"),
        P(None, "dp", "head"),
        P(None, "dp", "head"),
        P(None, "dp", "head"),
        P("head", "dp"),
        P("head", "dp"),
        P("head", "dp"),
    )
    out_specs = (
        P("dp", None),
        P("dp", None),
        P(("dp", "head"), None),
        P(),
        P(None, "dp"),
        P(None, "dp"),
        P(None, "dp"),
        P(None, "dp", "head"),
        P(None, "dp", "head"),
        P(None, "dp", "head"),
        P("dp", "head"),
        P("dp", "head"),
        P("dp", "head"),
        P(None, ("dp", "head"), None),
        P(None, ("dp", "head"), None),
        P(None, ("dp", "head"), None),
        P(None, "head", "dp"),
        P(None, "head", "dp"),
        P(None, "head", "dp"),
        P(None, "dp", "head"),
        P(None, "dp", "head"),
        P(None, "dp", "head"),
        P("head", "dp"),
        P("head", "dp"),
        P("head", "dp"),
    )
    return jax.shard_map(
        per_device, mesh=mesh, in_specs=in_specs, out_specs=out_specs, check_vma=False
    )
```

time: 1750 us -> 380 us (0.22)
  waiting for transfers between devices: 1010 us -> 0.57 us
  Pallas kernels: 0 us -> 329 us
  matrix products: 275 us -> 0 us
  local copies, waits for them, and re-layouts: 197 us -> 26.4 us
  blocking collectives: 141 us -> 0 us
  other arithmetic: 83.7 us -> 13.7 us
  between operations: 23.9 us -> 3.02 us
    unnamed x19 -> x0, waiting for transfers between devices: 502 us -> none
    pallas_call x0 -> x3, Pallas kernels: none -> 329 us  [the longest x1 128 us: gather_weights(): pl.pallas_call(functools.partial(gather_kernel, bits), out_shape=(jax.Sha...]
    reduce_scatter x3 -> x0, waiting for transfers between devices: 312 us -> none  [the longest x1 145 us: per_device(): lax.psum_scatter(grad_mlp_input, 'dp', scatter_dimension=1, tiled=True)]
    dot_general x108 -> x0, matrix products: 275 us -> none  [the longest x24 52.7 us: masked_scores(): jnp.einsum('qd,kd->qk', query_head, key_head, preferred_element_type=jnp....]
    all_gather x5 -> x0, waiting for transfers between devices: 149 us -> none  [the longest x1 68.7 us: per_device(): lax.all_gather(mlp_input.astype(jnp.bfloat16), 'dp', axis=1, tiled=True)]
    all_gather x2 -> x0, blocking collectives: 87.3 us -> none  [the longest x1 44.9 us: per_device(): lax.all_gather(query_cross.astype(jnp.bfloat16), 'dp', axis=0, tiled=True)]
    another operation x31 -> x3, local copies, waits for them, and re-layouts: 55.3 us -> 0.87 us  [the longest x1 0.74 us: unpack_grads(): keyval = jnp.stack([cut(CKV + i * HALF, HALF) for i in range(2)])]
    psum x5 -> x0, waiting for transfers between devices: 49 us -> none  [head_total(): lax.psum(partial_value.astype(jnp.bfloat16), 'head').astype(jnp.float32)]
  transfers between devices with their start and end apart: 16 -> 2, of which waited for: 13 -> 1; matrix products, arithmetic and copies ran while one was open for 12% -> 1% of each run, Pallas kernels for 0% -> 0%
where the time goes in v1:
time: 380 us; the launch traced here: 379 us
  Pallas kernels  329 us (87%)
  local copies, waits for them, and re-layouts  26.4 us (7%)
  other arithmetic  13.7 us (4%)
  starting transfers between devices  6.86 us (2%)
    pallas_call x1, Pallas kernels, gather_weights(): pl.pallas_call(functools.partial(gather_kernel, bits), out_shape=(jax.Sha...  128 us
    pallas_call x1, Pallas kernels, scatter_grads(): pl.pallas_call(functools.partial(scatter_kernel, bits), out_shape=(jax.Sh...  110 us
    pallas_call x1, Pallas kernels, layer(): pl.pallas_call(layer_kernel, out_shape=(jax.ShapeDtypeStruct((rows, D), B...  90.7 us
    unnamed x90, local copies, waits for them, and re-layouts  20.5 us
  transfers between devices with their start and end apart: 2, of which 1 were waited for; matrix products, arithmetic and copies ran while one was open for 1% of the time, Pallas kernels for 0%

profile of v1, /device:TPU:0, one launch (start us, length us, event | category | flops | bytes accessed | tf_op | source)
XLA Modules:
  0.0 379.0 jit_solution(8676940868874497058)
XLA Ops:
  0.7 1.0 convert_element_type.50
  2.1 1.1 reshape.119
  3.2 3.4 all-to-all-start
  6.7 1.0 convert.37
  8.4 0.6 constant_dynamic-update-slice_fusion.19
  9.0 0.6 constant_dynamic-update-slice_fusion.18
  9.6 0.6 constant_dynamic-update-slice_fusion.17
  11.2 0.6 constant_dynamic-update-slice_fusion.16
  11.8 0.6 constant_dynamic-update-slice_fusion.15
  12.4 0.6 constant_dynamic-update-slice_fusion.14
  13.0 0.6 constant_dynamic-update-slice_fusion.13
  13.7 0.6 constant_dynamic-update-slice_fusion.12
  14.4 0.6 constant_dynamic-update-slice_fusion.11
  15.0 0.6 constant_dynamic-update-slice_fusion.10
  15.6 0.6 constant_dynamic-update-slice_fusion.9
  16.2 0.6 constant_dynamic-update-slice_fusion.8
  16.8 0.6 constant_dynamic-update-slice_fusion.7
  17.4 0.6 constant_dynamic-update-slice_fusion.6
  18.0 0.6 constant_dynamic-update-slice_fusion.5
  18.7 0.6 constant_dynamic-update-slice_fusion.4
  19.3 0.6 constant_dynamic-update-slice_fusion.3
  19.9 0.6 constant_dynamic-update-slice_fusion.2
  20.5 0.6 constant_dynamic-update-slice_fusion.1
  21.1 0.6 constant_dynamic-update-slice_fusion.pack_ref
  21.8 127.7 %gather.1 = (bf16[2,2,2,2,48,6272]{5,4,3,2,1,0:T(8,128)(2,1)}, bf16[2,1024,768]{2,1,0:T(8,128)(2,1)}) custom-call(bf16[48,6272]{1,0:T(8,128)(2,1)} %constant_dynamic-update-slice_fusion.pack_ref, bf16[1024,768]{1,0:T(8,128)(2,1)} %mem_ref.1), custom_call_target="tpu_custom_call" | custom-call | tf_op jit(solution)/shard_map/gather/pallas_call | solution.py:187
  149.5 1.5 select_convert_fusion
  151.0 0.9 pad.11.cbias
  151.9 0.8 select_convert_fusion.1.sbias
  152.7 90.7 %layer.1 = (bf16[512,768]{1,0:T(8,128)(2,1)}, f32[512,768]{1,0:T(8,128)}, f32[1024,768]{1,0:T(8,128)}, bf16[768,6272]{1,0:T(8,128)(2,1)}) custom-call(bf16[512,768]{1,0:T(8,128)(2,1)} %tok.1, bf16[2048,768]{1,0:T(8,128)(2,1)} %bitcast.83, bf16[512,768]{1,0:T(8,128)(2,1)} %cot.1, bf16[2048,128]{1,0:T(8,128)(2,1)} %pad.11.cbias, ...), custom_call_target="tpu_custom_call" | custom-call | tf_op jit(solution)/shard_map/layer/pallas_call | solution.py:606
  243.5 110.2 %scatter.1 = (f32[48,6272]{1,0:T(8,128)}, f32[8,128]{1,0:T(8,128)}) custom-call(bf16[2,2,2,2,48,6272]{5,4,3,2,1,0:T(8,128)(2,1)} %bitcast.81), custom_call_target="tpu_custom_call" | custom-call | tf_op jit(solution)/shard_map/scatter/pallas_call | solution.py:714
  353.7 1.3 slice.175
  355.7 1.9 slice_bitcast_fusion.1
  357.6 0.7 copy.97
  358.4 3.4 all-to-all-start.1
  361.8 0.8 fusion.19
  364.0 0.7 copy.99
  364.7 0.7 copy.100
  365.3 0.7 copy.101
  366.0 1.8 multiply_subtract_fusion.4
  367.8 1.0 maximum_bitcast_fusion
  368.9 1.2 multiply_subtract_fusion
  370.1 0.8 multiply_subtract_fusion.3
  371.0 0.9 multiply_subtract_fusion.1
  372.0 0.9 multiply_subtract_fusion.2
  372.9 0.9 copy.125
  373.8 1.1 copy.126
  374.9 1.3 copy-done
  376.2 1.7 copy.127
  (91 shorter events, 3.6 us)
Async XLA Ops:
  0.7 7.0 %copy-start.24 = (f32[3,48]{1,0:T(4,128)S(1)}, f32[3,48]{1,0:T(4,128)}, u32[]{:S(2)}) copy-start(f32[3,48]{1,0:T(4,128)} %param.35) | copy-start | bytes 1732
  0.7 10.5 %copy-start.7 = (f32[2,384,48]{1,2,0:T(8,128)S(1)}, f32[2,384,48]{1,2,0:T(8,128)}, u32[]{:S(2)}) copy-start(f32[2,384,48]{1,2,0:T(8,128)} %param.47) | copy-start | bytes 442372
  1.6 11.4 %copy-start.12 = (f32[48,384]{1,0:T(8,128)S(1)}, f32[48,384]{1,0:T(8,128)}, u32[]{:S(2)}) copy-start(f32[48,384]{1,0:T(8,128)} %param.41) | copy-start | bytes 221188
  2.1 12.2 %copy-start.3 = (f32[2,48,1024]{2,1,0:T(8,128)S(1)}, f32[2,48,1024]{2,1,0:T(8,128)}, u32[]{:S(2)}) copy-start(f32[2,48,1024]{2,1,0:T(8,128)} %param.50) | copy-start | bytes 1179652
  3.2 11.1 %copy-start.5 = (f32[1024,48]{0,1:T(8,128)S(1)}, f32[1024,48]{0,1:T(8,128)}, u32[]{:S(2)}) copy-start(f32[1024,48]{0,1:T(8,128)} %param.53) | copy-start | bytes 589828
  3.2 7.0 %all-to-all-start = ((bf16[2,2,9216]{2,1,0:T(2,128)(2,1)}), bf16[2,2,9216]{2,1,0:T(2,128)(2,1)S(1)}, u32[]{:S(2)}, u32[]{:S(2)}) async-start(bf16[2,2,9216]{2,1,0:T(2,128)(2,1)} %reshape.119), calls=%async_computation | async-start | bytes 147456 | tf_op jit(solution)/shard_map/all_to_all | solution.py:787
  9.0 12.7 %copy-start.26 = (s32[2048]{0:T(1024)S(1)}, s32[2048]{0:T(1024)}, u32[]{:S(2)}) copy-start(s32[2048]{0:T(1024)} %param.32) | copy-start | bytes 24580
  9.0 12.7 %copy-start.30 = (s32[2]{0:T(128)S(1)}, s32[2]{0:T(128)}, u32[]{:S(2)}) copy-start(s32[2]{0:T(128)} %param.34) | copy-start | bytes 28
  14.3 135.1 %copy-start.25 = (s32[2048]{0:T(1024)S(1)}, s32[2048]{0:T(1024)}, u32[]{:S(2)}) copy-start(s32[2048]{0:T(1024)} %param.31) | copy-start | bytes 24580
  14.3 135.1 %copy-start.29 = (s32[2]{0:T(128)S(1)}, s32[2]{0:T(128)}, u32[]{:S(2)}) copy-start(s32[2]{0:T(128)} %param.33) | copy-start | bytes 28
  243.4 112.3 %copy-start.22 = (f32[48,384]{1,0:T(8,128)S(1)}, f32[48,384]{1,0:T(8,128)}, u32[]{:S(2)}) copy-start(f32[48,384]{1,0:T(8,128)} %param.43) | copy-start | bytes 221188
  243.4 112.3 %copy-start.23 = (f32[48,384]{1,0:T(8,128)S(1)}, f32[48,384]{1,0:T(8,128)}, u32[]{:S(2)}) copy-start(f32[48,384]{1,0:T(8,128)} %param.42) | copy-start | bytes 221188
  353.7 8.2 %copy-start.2 = (f32[48,6272]{1,0:T(8,128)S(1)}, f32[48,6272]{1,0:T(8,128)}, u32[]{:S(2)}) copy-start(f32[48,6272]{1,0:T(8,128)} %get-tuple-element.40) | copy-start | bytes 3612676
  357.6 5.9 %copy-start.27 = (f32[3,48]{1,0:T(4,128)S(1)}, f32[3,48]{1,0:T(4,128)}, u32[]{:S(2)}) copy-start(f32[3,48]{1,0:T(4,128)} %param.36) | copy-start | bytes 1732
  357.6 6.0 %copy-start.28 = (f32[3,48]{1,0:T(4,128)S(1)}, f32[3,48]{1,0:T(4,128)}, u32[]{:S(2)}) copy-start(f32[3,48]{1,0:T(4,128)} %param.37) | copy-start | bytes 1732
  357.6 8.4 %copy-start.8 = (f32[2,24,768]{2,1,0:T(8,128)S(1)}, f32[2,24,768]{2,1,0:T(8,128)}, u32[]{:S(2)}) copy-start(f32[2,24,768]{2,1,0:T(8,128)} %param.44) | copy-start | bytes 442372
  358.4 4.9 %all-to-all-start.1 = ((f32[2,48,384]{2,0,1:T(2,128)}), f32[2,48,384]{2,0,1:T(2,128)S(1)}, u32[]{:S(2)}, u32[]{:S(2)}) async-start(f32[2,48,384]{2,0,1:T(2,128)} %copy.97), calls=%async_computation.1 | async-start | bytes 294912 | tf_op jit(solution)/shard_map/all_to_all | solution.py:808
  363.3 5.6 %copy-start.9 = (f32[2,48,1024]{2,1,0:T(8,128)S(1)}, f32[2,48,1024]{2,1,0:T(8,128)}, u32[]{:S(2)}) copy-start(f32[2,48,1024]{2,1,0:T(8,128)} %param.51) | copy-start | bytes 1179652
  363.3 5.6 %copy-start.10 = (f32[2,48,1024]{2,1,0:T(8,128)S(1)}, f32[2,48,1024]{2,1,0:T(8,128)}, u32[]{:S(2)}) copy-start(f32[2,48,1024]{2,1,0:T(8,128)} %param.52) | copy-start | bytes 1179652
  368.8 1.3 copy-start.11
  368.8 1.3 copy-start.20
  368.8 1.3 copy-start.21
  368.8 2.1 copy-start.4
  368.9 2.1 copy-start.13
  368.9 2.1 copy-start.14
  370.1 1.9 copy-start.15
  370.1 1.9 copy-start.16
  370.1 1.9 copy-start.17
  370.1 1.9 copy-start.18
  370.1 1.9 copy-start.19
  371.0 1.9 copy-start.6
  371.9 1.8 copy-start.1
  373.8 2.5 copy-start
